TPU v7x, 32 devices: a whole 2x2x4 slice. The times are simulated.
32 devices in a mesh: op: 8 (over y, x, core), sec: 4 (over z).
Axes of the slice: x: 2, y: 2, z: 4, core: 2. Of those that a mesh axis runs over, the one named last changes fastest.
Arguments:
- wave: bfloat16 [32, 256, 4, 256], P('op'), may hold values from -6 to 6
- sector_dims: int32 [32], replicated, may hold values from 64 to 256, as said below
- left_ops: bfloat16 [32, 32, 256, 256], P(None, ('op', 'sec')), may hold values from -0.375 to 0.375
- right_ops: bfloat16 [32, 8, 4, 256, 256], P('op', None, 'sec'), may hold values from -0.375 to 0.375
- site_ops: float32 [32, 4, 4], replicated, may hold values from -0.5 to 0.5
Outputs:
- sigma: bfloat16 [32, 256, 4, 256], P('op', 'sec')
Inputs may be any that keep to these rules, and one draw needn't show every extreme that they name: `sector_dims`: every entry is a multiple of 64, and at least one sector has exactly 256 states.
All inputs are finite; a program needn't handle non-finite values.
Results may differ from a plain program's by a relative error of at most 0.005.
Values may be sent and summed in bfloat16 or wider, within the bound.
A program may use at most 128 MiB of HBM per device.

v0:
```python
import jax
import jax.numpy as jnp
from jax import lax
from jax.sharding import PartitionSpec as P


def sector_mask(sizes, width):
    places = lax.broadcasted_iota(jnp.int32, (sizes.shape[0], width), 1)
    return (places < sizes[:, None]).astype(jnp.float32)


def left_step(blocks, waves, site_mats):

    def one_sector(inputs):
        ops_block, wave_block = inputs
        first = jnp.einsum(
            "klm,mpr->klpr", ops_block, wave_block, preferred_element_type=jnp.float32
        )
        second = jnp.einsum("klpr,kqp->klqr", first, site_mats, precision=lax.Precision.HIGHEST)
        return second.astype(jnp.bfloat16)

    return lax.map(one_sector, (blocks, waves))


def shards(wave, sector_dims, left_ops, right_ops, site_ops):
    sec_count = lax.axis_size("sec")
    op_index = lax.axis_index("op")
    sec_index = lax.axis_index("sec")
    local_sectors = wave.shape[0]
    width = wave.shape[1]
    term_count = left_ops.shape[1]
    own_sizes = lax.dynamic_slice_in_dim(sector_dims, op_index * local_sectors, local_sectors)
    own_mask = sector_mask(own_sizes, width)
    masked = (
        wave.astype(jnp.float32) * own_mask[:, :, None, None] * own_mask[:, None, None, :]
    ).astype(jnp.bfloat16)
    first_term = (op_index * sec_count + sec_index) * term_count
    site_local = lax.dynamic_slice_in_dim(site_ops, first_term, term_count)
    inter = left_step(left_ops, lax.all_gather(masked, "op", axis=0, tiled=True), site_local)
    inter = lax.all_to_all(inter, "op", split_axis=0, concat_axis=1, tiled=True)
    right_local = right_ops.reshape(local_sectors, -1, width, width)
    partial_sum = jnp.einsum(
        "sklqm,skrm->slqr", inter, right_local, preferred_element_type=jnp.float32
    )
    row_count = width // sec_count
    summed = lax.psum(partial_sum, "sec")
    share = lax.dynamic_slice_in_dim(summed, sec_index * row_count, row_count, 1)
    row_mask = lax.dynamic_slice_in_dim(own_mask, sec_index * row_count, row_count, 1)
    return (share * row_mask[:, :, None, None] * own_mask[:, None, None, :]).astype(jnp.bfloat16)


def solution(mesh):
    placed = (
        P("op", None, None, None),
        P(),
        P(None, ("op", "sec"), None, None),
        P("op", None, "sec", None, None),
        P(),
    )
    return jax.shard_map(
        shards, mesh=mesh, in_specs=placed, out_specs=P("op", "sec", None, None), check_vma=False
    )
```

profile of v0, /device:TPU:1, one launch (start us, length us, event | category | flops | bytes accessed | tf_op | source)
XLA Modules:
  0.0 629.4 jit_solution(15689383101245994761)
XLA Ops:
  7.4 3.5 multiply_convert_fusion
  11.1 92.3 %all-gather.2.cloned.1.call-done = bf16[32,256,4,256]{3,1,2,0:T(8,128)(2,1)} async-done(((bf16[4,256,4,256]{3,1,2,0:T(8,128)(2,1)}), bf16[32,256,4,256]{3,1,2,0:T(8,128)(2,1)}) %all-gather.2.cloned.1.call-update) | async-done | bytes 16777232 | tf_op jit(solution)/shard_map/all_gather | solution.py:39
  103.4 153.4 %while.10 = (s32[]{:T(128)}, bf16[32,1,256,4,256]{4,2,3,1,0:T(8,128)(2,1)}, bf16[32,1,256,256]{3,2,1,0:T(8,128)(2,1)}, bf16[32,256,4,256]{3,1,2,0:T(8,128)(2,1)}, f32[1,4,4]{2,1,0:T(4,128)S(1)}, /*index=5*/s32[]{:T(128)}) while((s32[]{:T(128)}, bf16[32,1,256,4,256]{4,2,3,1,0:T(8,128)(2,1)}, bf16[32,1,256,256]{3,2,1,0:T(8,128)(2,1)}, ...), condition=%wide.region_1.2_spmd, body=%wide.region_0.1_spmd.sunk | while | flops 147062784 | bytes 4327045 | solution.py:22
  104.8 2.5 fusion.25
  109.6 2.5 fusion.25
  114.4 2.5 fusion.25
  119.1 2.5 fusion.25
  123.9 2.5 fusion.25
  128.7 2.5 fusion.25
  133.5 2.5 fusion.25
  143.1 2.5 fusion.25
  147.9 2.5 fusion.25
  152.7 2.5 fusion.25
  157.5 2.5 fusion.25
  162.3 2.5 fusion.25
  176.6 2.5 fusion.25
  181.4 2.5 fusion.25
  186.3 2.5 fusion.25
  191.1 2.5 fusion.25
  200.6 2.5 fusion.25
  205.5 2.5 fusion.25
  210.2 2.5 fusion.25
  215.0 2.5 fusion.25
  219.8 2.5 fusion.25
  224.6 2.5 fusion.25
  234.2 2.5 fusion.25
  239.0 2.5 fusion.25
  253.4 2.5 fusion.25
  256.8 190.3 %all_to_all.18 = bf16[32,1,256,4,256]{4,2,3,1,0:T(8,128)(2,1)} all-to-all(bf16[32,1,256,4,256]{4,2,3,1,0:T(8,128)(2,1)} %get-tuple-element.32), channel_id=1, replica_groups=mesh['op'=8,'sec'=4] {'op'}, dimensions={0} | all-to-all | bytes 33554432 | tf_op jit(solution)/shard_map/all_to_all | solution.py:40
  447.1 13.4 %fusion.9 = f32[4,256,4,256,1]{3,1,2,0,4:T(8,128)} fusion(bf16[4,8,256,4,256]{4,2,3,0,1:T(8,128)(2,1)} %bitcast.43, bf16[4,8,1,256,256]{4,3,2,1,0:T(8,128)(2,1)} %param.10), kind=kOutput, calls=%fused_computation.11 | convolution fusion | flops 4294967296 | bytes 25165824 | tf_op jit(solution)/shard_map/sklqm,skrm->slqr/dot_general | solution.py:42
  460.5 4.5 copy.35
  465.2 154.8 %all-reduce.2.cloned.1.call-done = f32[4,256,4,256]{3,1,0,2:T(8,128)} async-done(((f32[4,256,4,256]{3,1,0,2:T(8,128)}), f32[4,256,4,256]{3,1,0,2:T(8,128)}) %all-reduce.2.cloned.1.call-update) | async-done | bytes 4194320 | tf_op jit(solution)/shard_map/psum | solution.py:46
  (87 shorter events, 94.6 us)
Async XLA Ops:
  6.5 4.4 copy-start
  6.5 96.8 %all-gather.2.cloned.1.call-start = ((), (), s32[]{:S(2)}) async-start(), calls=%async_computation.1 | async-start | bytes 18874368 | tf_op jit(solution)/shard_map/all_gather | solution.py:39
  10.9 609.1 %all-reduce.2.cloned.1.call-start = ((), (), s32[]{:S(2)}) async-start(), calls=%async_computation.2 | async-start | bytes 8388608 | tf_op jit(solution)/shard_map/psum | solution.py:46
  460.5 162.1 %copy-start.1 = (f32[32,4,4]{0,2,1:T(4,128)S(1)}, f32[32,4,4]{0,2,1:T(4,128)}, u32[]{:S(2)}) copy-start(f32[32,4,4]{0,2,1:T(4,128)} %param.11) | copy-start | bytes 6148
Sparse Core Ops, SparseCore 0:
  11.0 92.3 all-gather.1
  465.2 154.7 all-reduce.1
where the time goes:
time: 631 us; the launch traced here: 629 us
  waiting for transfers between devices  247 us (39%)
  blocking collectives  190 us (30%)
  matrix products  138 us (22%)
  local copies, waits for them, and re-layouts  34.9 us (6%)
  between operations  13.4 us (2%)
    all_to_all x1, blocking collectives, shards(): inter = lax.all_to_all(inter, 'op', split_axis=0, concat_axis=1, tiled=True)  190 us
    psum x1, waiting for transfers between devices, shards(): summed = lax.psum(partial_sum, 'sec')  155 us
    all_gather x1, waiting for transfers between devices, shards(): lax.all_gather(masked, 'op', axis=0, tiled=True)  92.3 us
    dot_general x32, matrix products, one_sector(): jnp.einsum('klpr,kqp->klqr', first, site_mats, precision=lax.Precision.HI...  79.6 us
    dot_general x32, matrix products, one_sector(): jnp.einsum('klm,mpr->klpr', ops_block, wave_block, preferred_element_type...  45.2 us
    dynamic_update_slice x32, local copies, waits for them, and re-layouts, left_step(): return lax.map(one_sector, (blocks, waves))  28.2 us
    dot_general x1, matrix products, shards(): jnp.einsum('sklqm,skrm->slqr', inter, right_local, preferred_element_type...  13.4 us
  transfers between devices with their start and end apart: 2, of which 2 were waited for; matrix products, arithmetic and copies ran while one was open for 0% of the time, Pallas kernels for 0%

commit v1 on v0

v1 whole, which is shorter than its diff:
```python
import functools

import jax
import jax.numpy as jnp
from jax import lax
from jax.experimental import pallas as pl
from jax.experimental.pallas import tpu as pltpu
from jax.sharding import PartitionSpec as P

MESH = pl.DeviceIdType.MESH
MIB = 1024 * 1024


def sector_mask(sizes, width):
    places = lax.broadcasted_iota(jnp.int32, (sizes.shape[0], width), 1)
    return (places < sizes[:, None]).astype(jnp.float32)


def kernel(
    n_op, n_sec, site_ref, psi_hbm, left_hbm, right_hbm, out_ref,
    psi, right, left, mixed, total, zsend, zrecv,
    psi_sem, right_sem, own_sem, lsend_sem, lrecv_sem, zsend_sem, zrecv_sem,
):
    o = lax.axis_index("op")
    z = lax.axis_index("sec")
    sectors, p_size, width = psi.shape[0], psi.shape[1], psi.shape[2]
    rows = width // n_sec
    chunk = width // 4

    def psi_copy(j):
        return pltpu.make_async_copy(psi_hbm.at[j], psi.at[j], psi_sem.at[j])

    def right_copy(j):
        return pltpu.make_async_copy(right_hbm.at[j], right.at[j], right_sem.at[j])

    def own_copy(j):
        return pltpu.make_async_copy(left_hbm.at[o, j], left.at[j, o], own_sem.at[j])

    def left_out(j, peer):
        return pltpu.make_async_remote_copy(
            src_ref=left_hbm.at[peer, j], dst_ref=left.at[j, o],
            send_sem=lsend_sem.at[j, peer], recv_sem=lrecv_sem.at[j, o],
            device_id=(peer, z), device_id_type=MESH,
        )

    def left_in(j, peer):
        return pltpu.make_async_remote_copy(
            src_ref=left_hbm.at[peer, j], dst_ref=left.at[j, peer],
            send_sem=lsend_sem.at[j, peer], recv_sem=lrecv_sem.at[j, peer],
            device_id=(peer, z), device_id_type=MESH,
        )

    def part_out(j, peer):
        return pltpu.make_async_remote_copy(
            src_ref=zsend.at[j, pl.ds(pl.multiple_of(peer * rows, rows), rows)],
            dst_ref=zrecv.at[j, z],
            send_sem=zsend_sem.at[j, peer], recv_sem=zrecv_sem.at[j, z],
            device_id=(o, peer), device_id_type=MESH,
        )

    def part_in(j, peer):
        return pltpu.make_async_remote_copy(
            src_ref=zsend.at[j, pl.ds(pl.multiple_of(peer * rows, rows), rows)],
            dst_ref=zrecv.at[j, peer],
            send_sem=zsend_sem.at[j, peer], recv_sem=zrecv_sem.at[j, peer],
            device_id=(o, peer), device_id_type=MESH,
        )

    def op_peers(body):
        def step(i, _):
            body(lax.rem(o + i, n_op))
            return 0
        lax.fori_loop(1, n_op, step, 0)

    def sec_peers(body):
        def step(i, _):
            body(lax.rem(z + i, n_sec))
            return 0
        lax.fori_loop(1, n_sec, step, 0)

    barrier = pltpu.get_barrier_semaphore()
    op_peers(lambda peer: pl.semaphore_signal(
        barrier, inc=1, device_id=(peer, z), device_id_type=MESH))
    sec_peers(lambda peer: pl.semaphore_signal(
        barrier, inc=1, device_id=(o, peer), device_id_type=MESH))
    for j in range(sectors):
        psi_copy(j).start()
        right_copy(j).start()
        own_copy(j).start()
    pl.semaphore_wait(barrier, n_op + n_sec - 2)

    for j in range(sectors):
        op_peers(lambda peer: left_out(j, peer).start())

    def mix(j):
        psi_copy(j).wait()
        right_copy(j).wait()

        def one_term(a, _):
            block = right[j, a]
            term = a * n_sec + z
            weights = [[site_ref[term, q, p] for p in range(p_size)] for q in range(p_size)]
            for c in range(width // chunk):
                here = pl.ds(c * chunk, chunk)
                waves = psi[j, :, here, :].reshape(p_size * chunk, width)
                got = lax.dot_general(
                    waves, block, (((1,), (1,)), ((), ())), preferred_element_type=jnp.float32
                )
                for q in range(p_size):
                    value = weights[q][0] * got[:chunk]
                    for p in range(1, p_size):
                        value = value + weights[q][p] * got[p * chunk:(p + 1) * chunk]
                    mixed[j, a, here, pl.ds(q * width, width)] = value.astype(jnp.bfloat16)
            return 0

        lax.fori_loop(0, n_op, one_term, 0)

    def contract(j):
        own_copy(j).wait()
        op_peers(lambda peer: left_in(j, peer).wait_recv())

        def one_state(q, _):
            cols = pl.ds(pl.multiple_of(q * width, width), width)
            value = jnp.dot(left[j, 0], mixed[j, 0, :, cols], preferred_element_type=jnp.float32)
            for a in range(1, n_op):
                value = value + jnp.dot(
                    left[j, a], mixed[j, a, :, cols], preferred_element_type=jnp.float32
                )
            total[j, :, cols] = value
            zsend[j, :, cols] = value.astype(jnp.bfloat16)
            return 0

        lax.fori_loop(0, p_size, one_state, 0)
        sec_peers(lambda peer: part_out(j, peer).start())

    mix(0)
    for j in range(sectors):
        if j + 1 < sectors:
            mix(j + 1)
        contract(j)

    for j in range(sectors):
        sec_peers(lambda peer: part_in(j, peer).wait_recv())
        value = total[j, pl.ds(pl.multiple_of(z * rows, rows), rows), :]
        for i in range(1, n_sec):
            value = value + zrecv[j, lax.rem(z + i, n_sec)].astype(jnp.float32)
        out_ref[j] = value.astype(jnp.bfloat16)

    for j in range(sectors):
        op_peers(lambda peer: left_out(j, peer).wait_send())
        sec_peers(lambda peer: part_out(j, peer).wait_send())


def shards(wave, sector_dims, left_ops, right_ops, site_ops):
    n_op = lax.axis_size("op")
    n_sec = lax.axis_size("sec")
    o = lax.axis_index("op")
    z = lax.axis_index("sec")
    sectors, width, p_size = wave.shape[0], wave.shape[1], wave.shape[2]
    rows = width // n_sec
    own_sizes = lax.dynamic_slice_in_dim(sector_dims, o * sectors, sectors)
    own_mask = sector_mask(own_sizes, width)
    masked = (
        wave.astype(jnp.float32) * own_mask[:, :, None, None] * own_mask[:, None, None, :]
    ).astype(jnp.bfloat16)
    masked = jnp.transpose(masked, (0, 2, 1, 3))
    left = left_ops.reshape(n_op, sectors, width, width)
    right = right_ops.reshape(sectors, n_op, width, width)
    wide = p_size * width
    flops = 4 * sectors * n_op * width * width * wide
    partial = pl.pallas_call(
        functools.partial(kernel, n_op, n_sec),
        out_shape=jax.ShapeDtypeStruct((sectors, rows, wide), jnp.bfloat16),
        in_specs=[
            pl.BlockSpec(memory_space=pltpu.SMEM),
            pl.BlockSpec(memory_space=pl.ANY),
            pl.BlockSpec(memory_space=pl.ANY),
            pl.BlockSpec(memory_space=pl.ANY),
        ],
        out_specs=pl.BlockSpec(memory_space=pltpu.VMEM),
        scratch_shapes=[
            pltpu.VMEM((sectors, p_size, width, width), jnp.bfloat16),
            pltpu.VMEM((sectors, n_op, width, width), jnp.bfloat16),
            pltpu.VMEM((sectors, n_op, width, width), jnp.bfloat16),
            pltpu.VMEM((sectors, n_op, width, wide), jnp.bfloat16),
            pltpu.VMEM((sectors, width, wide), jnp.float32),
            pltpu.VMEM((sectors, width, wide), jnp.bfloat16),
            pltpu.VMEM((sectors, n_sec, rows, wide), jnp.bfloat16),
            pltpu.SemaphoreType.DMA((sectors,)),
            pltpu.SemaphoreType.DMA((sectors,)),
            pltpu.SemaphoreType.DMA((sectors,)),
            pltpu.SemaphoreType.DMA((sectors, n_op)),
            pltpu.SemaphoreType.DMA((sectors, n_op)),
            pltpu.SemaphoreType.DMA((sectors, n_sec)),
            pltpu.SemaphoreType.DMA((sectors, n_sec)),
        ],
        compiler_params=pltpu.CompilerParams(
            collective_id=0, has_side_effects=True, vmem_limit_bytes=48 * MIB
        ),
        cost_estimate=pl.CostEstimate(flops=flops, bytes_accessed=12 * MIB, transcendentals=0),
    )(site_ops, masked, left, right)
    row_mask = lax.dynamic_slice_in_dim(own_mask, z * rows, rows, 1)
    sigma = partial.reshape(sectors, rows, p_size, width).astype(jnp.float32)
    return (sigma * row_mask[:, :, None, None] * own_mask[:, None, None, :]).astype(jnp.bfloat16)


def solution(mesh):
    placed = (
        P("op", None, None, None),
        P(),
        P(None, ("op", "sec"), None, None),
        P("op", None, "sec", None, None),
        P(),
    )
    return jax.shard_map(
        shards, mesh=mesh, in_specs=placed, out_specs=P("op", "sec", None, None), check_vma=False
    )
```

time: 631 us -> 72.5 us (0.11)
  waiting for transfers between devices: 247 us -> 0 us
  blocking collectives: 190 us -> 0 us
  matrix products: 138 us -> 0 us
  Pallas kernels: 0 us -> 66.5 us
  local copies, waits for them, and re-layouts: 34.9 us -> 2.07 us
  between operations: 13.4 us -> 0.04 us
    all_to_all x1 -> x0, blocking collectives: 190 us -> none  [shards(): inter = lax.all_to_all(inter, 'op', split_axis=0, concat_axis=1, tiled=True)]
    psum x1 -> x0, waiting for transfers between devices: 155 us -> none  [shards(): summed = lax.psum(partial_sum, 'sec')]
    dot_general x65 -> x0, matrix products: 138 us -> none  [the longest x32 79.6 us: one_sector(): jnp.einsum('klpr,kqp->klqr', first, site_mats, precision=lax.Precision.HI...]
    all_gather x1 -> x0, waiting for transfers between devices: 92.3 us -> none  [shards(): lax.all_gather(masked, 'op', axis=0, tiled=True)]
    pallas_call x0 -> x1, Pallas kernels: none -> 66.5 us  [shards(): pl.pallas_call(functools.partial(kernel, n_op, n_sec), out_shape=jax.Shap...]
    dynamic_update_slice x32 -> x0, local copies, waits for them, and re-layouts: 28.2 us -> none  [left_step(): return lax.map(one_sector, (blocks, waves))]
  transfers between devices with their start and end apart: 2 -> 0, of which waited for: 2 -> 0; matrix products, arithmetic and copies ran while one was open for 0% -> 0% of each run, Pallas kernels for 0% -> 0%
where the time goes in v1:
time: 72.5 us; the launch traced here: 72 us
  Pallas kernels  66.5 us (92%)
  other arithmetic  3.34 us (5%)
  local copies, waits for them, and re-layouts  2.07 us (3%)
    pallas_call x1, Pallas kernels, shards(): pl.pallas_call(functools.partial(kernel, n_op, n_sec), out_shape=jax.Shap...  66.5 us
    transpose x1, other arithmetic, shards(): masked = jnp.transpose(masked, (0, 2, 1, 3))  2.13 us

profile of v1, /device:TPU:1, one launch (start us, length us, event | category | flops | bytes accessed | tf_op | source)
XLA Modules:
  0.0 72.0 jit_solution(8202765693486070550)
XLA Ops:
  0.0 0.8 %copy.7.site_ref = f32[32,4,4]{2,1,0:T(4,128)S(1)} copy(f32[32,4,4]{0,2,1:T(4,128)} %param.9) | data formatting | bytes 4096 | tf_op args[4]
  0.8 0.7 %dynamic_slice.6 = s32[4]{0:T(128)S(1)} dynamic-slice(s32[32]{0:T(128)} %param.6, s32[]{:T(128)S(6)} %select_n.6), dynamic_slice_sizes={4} | dynamic-slice | bytes 36 | tf_op jit(solution)/shard_map/dynamic_slice | solution.py:161
  1.5 0.1 fusion.1
  1.6 2.1 %fusion.psi_hbm = bf16[4,4,256,256]{3,2,1,0:T(8,128)(2,1)S(1)} fusion(bf16[4,256,4,256]{3,2,1,0:T(4,128)(2,1)} %param.5, f32[4,256]{1,0:T(4,128)S(1)} %fusion.1), kind=kLoop, calls=%fused_computation.1 | loop fusion | flops 4194304 | bytes 4198400 | tf_op jit(solution)/shard_map/transpose | solution.py:166
  3.8 66.5 %shard_map.55 = bf16[4,64,1024]{2,1,0:T(8,128)(2,1)S(1)} custom-call(f32[32,4,4]{2,1,0:T(4,128)S(1)} %copy.7.site_ref, bf16[4,4,256,256]{3,2,1,0:T(8,128)(2,1)S(1)} %fusion.psi_hbm, bf16[8,4,256,256]{3,2,1,0:T(8,128)(2,1)} %bitcast.4, bf16[4,8,256,256]{3,2,1,0:T(8,128)(2,1)} %bitcast.5), custom_call_target="tpu_custom_call" | custom-call | flops 8589934592 | bytes 12582912 | tf_op jit(solution)/shard_map/pallas_call | solution.py:171
  70.3 0.5 reshape.46
  70.8 0.1 constant_dynamic-slice_fusion
  70.9 1.1 %multiply_convert_fusion.1 = bf16[4,64,4,256]{3,2,1,0:T(4,128)(2,1)} fusion(f32[4,64,4,256]{3,2,1,0:T(4,128)S(1)} %reshape.46, f32[4,256]{1,0:T(4,128)S(1)} %fusion.1, f32[4,64]{1,0:T(4,128)S(1)} %constant_dynamic-slice_fusion), kind=kLoop, calls=%fused_computation.2 | loop fusion | flops 786432 | bytes 1577984 | tf_op jit(solution)/shard_map/convert_element_type | solution.py:204

commit v2 on v1

v2 whole, which is shorter than its diff:
```python
import functools

import jax
import jax.numpy as jnp
from jax import lax
from jax.experimental import pallas as pl
from jax.experimental.pallas import tpu as pltpu
from jax.sharding import PartitionSpec as P

MESH = pl.DeviceIdType.MESH
MIB = 1024 * 1024


def kernel(
    n_op, n_sec, site_ref, dims_ref, psi_hbm, left_hbm, right_hbm, out_ref,
    psi, right, left, mixed, total, zsend, zrecv, relayed,
    psi_sem, right_sem, own_sem, lsend_sem, lrecv_sem, zsend_sem, zrecv_sem, relay_sem,
):
    o = lax.axis_index("op")
    z = lax.axis_index("sec")
    sectors, p_size, width = psi.shape[0], psi.shape[1], psi.shape[2]
    rows = width // n_sec
    chunk = width // 4
    relays = n_sec == 4

    if relays:
        half = z // 2
        beside = z + 1 - 2 * lax.rem(z, 2)
        far = 3 * (1 - half)
        order = [far, 2 - half, beside, z]
        outer = lax.rem(z, 3) == 0
    else:
        order = [lax.rem(z + i, n_sec) for i in range(1, n_sec + 1)]

    def units_of(j):
        if j == sectors - 1:
            parts = 4
        elif j == 0:
            parts = 2
        else:
            return [None]
        each = n_sec // parts
        return [order[i * each:(i + 1) * each] for i in range(parts)]

    def psi_copy(j):
        return pltpu.make_async_copy(psi_hbm.at[j], psi.at[j], psi_sem.at[j])

    def right_copy(j):
        return pltpu.make_async_copy(right_hbm.at[j], right.at[j], right_sem.at[j])

    def own_copy(j):
        return pltpu.make_async_copy(left_hbm.at[o, j], left.at[j, o], own_sem.at[j])

    def rows_of(block):
        if block is None:
            return pl.ds(0, width)
        return pl.ds(pl.multiple_of(block * rows, rows), rows)

    def left_copy(j, block, peer, slot):
        which = 0 if block is None else block
        return pltpu.make_async_remote_copy(
            src_ref=left_hbm.at[peer, j, rows_of(block)],
            dst_ref=left.at[j, slot, rows_of(block)],
            send_sem=lsend_sem.at[j, which, peer], recv_sem=lrecv_sem.at[j, which, slot],
            device_id=(peer, z), device_id_type=MESH,
        )

    def part_copy(j, peer, slot):
        return pltpu.make_async_remote_copy(
            src_ref=zsend.at[j, rows_of(peer)], dst_ref=zrecv.at[j, slot],
            send_sem=zsend_sem.at[j, peer], recv_sem=zrecv_sem.at[j, slot],
            device_id=(o, peer), device_id_type=MESH,
        )

    def relay_copy(j):
        return pltpu.make_async_remote_copy(
            src_ref=zsend.at[j, rows_of(far)], dst_ref=relayed.at[j],
            send_sem=zsend_sem.at[j, far], recv_sem=relay_sem.at[j],
            device_id=(o, beside), device_id_type=MESH,
        )

    def op_peers(body):
        def step(i, _):
            body(lax.rem(o + i, n_op))
            return 0
        lax.fori_loop(1, n_op, step, 0)

    def sec_peers(body):
        def step(i, _):
            body(lax.rem(z + i, n_sec))
            return 0
        lax.fori_loop(1, n_sec, step, 0)

    def left_blocks(j):
        return [block for unit in units_of(j) for block in (unit or [None])]

    barrier = pltpu.get_barrier_semaphore()
    op_peers(lambda peer: pl.semaphore_signal(
        barrier, inc=1, device_id=(peer, z), device_id_type=MESH))
    sec_peers(lambda peer: pl.semaphore_signal(
        barrier, inc=1, device_id=(o, peer), device_id_type=MESH))
    for j in range(sectors):
        psi_copy(j).start()
        right_copy(j).start()
        own_copy(j).start()
    pl.semaphore_wait(barrier, n_op + n_sec - 2)

    for j in range(sectors):
        for block in left_blocks(j):
            op_peers(lambda peer: left_copy(j, block, peer, o).start())

    def mask_of(j, first, height):
        size = dims_ref[o * sectors + j]
        down = lax.broadcasted_iota(jnp.int32, (height, width), 0) + first
        across = lax.broadcasted_iota(jnp.int32, (height, width), 1)
        return jnp.where((down < size) & (across < size), 1.0, 0.0).astype(jnp.float32)

    def mix(j):
        psi_copy(j).wait()
        right_copy(j).wait()
        inside = mask_of(j, 0, width).astype(jnp.bfloat16)
        for p in range(p_size):
            psi[j, p] = psi[j, p] * inside

        def one_term(a, _):
            block = right[j, a]
            term = a * n_sec + z
            weights = [[site_ref[q, p, term] for p in range(p_size)] for q in range(p_size)]
            for c in range(width // chunk):
                here = pl.ds(c * chunk, chunk)
                waves = psi[j, :, here, :].reshape(p_size * chunk, width)
                got = lax.dot_general(
                    waves, block, (((1,), (1,)), ((), ())), preferred_element_type=jnp.float32
                )
                for q in range(p_size):
                    value = weights[q][0] * got[:chunk]
                    for p in range(1, p_size):
                        value = value + weights[q][p] * got[p * chunk:(p + 1) * chunk]
                    mixed[j, a, here, pl.ds(q * width, width)] = value.astype(jnp.bfloat16)
            return 0

        lax.fori_loop(0, n_op, one_term, 0)

    def send_part(j, block):
        if not relays:
            part_copy(j, block, z).start()
        elif block is far:
            @pl.when(outer)
            def _():
                relay_copy(j).start()
        else:
            part_copy(j, block, z).start()

    def relay(j):
        if not relays:
            return

        @pl.when(jnp.logical_not(outer))
        def _():
            relay_copy(j).wait_recv()
            value = total[j, rows_of(far), :] + relayed[j].astype(jnp.float32)
            zsend[j, rows_of(far), :] = value.astype(jnp.bfloat16)
            part_copy(j, far, z).start()

    def contract(j, unit):
        blocks = unit or [None]
        for block in blocks:
            op_peers(lambda peer: left_copy(j, block, peer, peer).wait_recv())

        def left_rows(a):
            parts = [left[j, a, rows_of(block), :] for block in blocks]
            return parts[0] if len(parts) == 1 else jnp.concatenate(parts, axis=0)

        def one_state(q, _):
            cols = pl.ds(pl.multiple_of(q * width, width), width)
            value = jnp.dot(
                left_rows(0), mixed[j, 0, :, cols], preferred_element_type=jnp.float32
            )
            for a in range(1, n_op):
                value = value + jnp.dot(
                    left_rows(a), mixed[j, a, :, cols], preferred_element_type=jnp.float32
                )
            height = value.shape[0] // len(blocks)
            for i, block in enumerate(blocks):
                part = value[i * height:(i + 1) * height]
                total[j, rows_of(block), cols] = part
                zsend[j, rows_of(block), cols] = part.astype(jnp.bfloat16)
            return 0

        lax.fori_loop(0, p_size, one_state, 0)
        for block in (unit or order):
            if block is not order[-1]:
                send_part(j, block)

    def finish(j):
        own = rows_of(z)
        inside = mask_of(j, z * rows, rows)
        if relays:
            part_copy(j, 2 - half, 2 - half).wait_recv()
            part_copy(j, beside, beside).wait_recv()

            @pl.when(jnp.logical_not(outer))
            def _():
                part_copy(j, far, far).wait_recv()
                total[j, own, :] = total[j, own, :] + zrecv[j, far].astype(jnp.float32)

            peers = [2 - half, beside]
        else:
            sec_peers(lambda peer: part_copy(j, peer, peer).wait_recv())
            peers = order[:-1]
        for q in range(p_size):
            cols = pl.ds(q * width, width)
            value = total[j, own, cols]
            for peer in peers:
                value = value + zrecv[j, peer, :, cols].astype(jnp.float32)
            out_ref[j, :, cols] = (value * inside).astype(jnp.bfloat16)

    mix(0)
    last = sectors - 1
    for j in range(sectors):
        if j < last:
            mix(j + 1)
        if j == last:
            for i in range(last - 1):
                finish(i)
        own_copy(j).wait()
        for i, unit in enumerate(units_of(j)):
            contract(j, unit)
            if i == 0 and j > 0:
                relay(j - 1)
            if i == 1 and j == last:
                relay(j)
    for j in range(max(last - 1, 0), sectors):
        finish(j)

    for j in range(sectors):
        for block in left_blocks(j):
            op_peers(lambda peer: left_copy(j, block, peer, o).wait_send())
        sec_peers(lambda peer: part_copy(j, peer, z).wait_send())


def shards(wave, sector_dims, left_ops, right_ops, site_ops):
    n_op = lax.axis_size("op")
    n_sec = lax.axis_size("sec")
    sectors, width, p_size = wave.shape[0], wave.shape[1], wave.shape[2]
    rows = width // n_sec
    waves = jnp.transpose(wave, (0, 2, 1, 3))
    left = left_ops.reshape(n_op, sectors, width, width)
    right = right_ops.reshape(sectors, n_op, width, width)
    sites = jnp.transpose(site_ops, (1, 2, 0))
    wide = p_size * width
    flops = 4 * sectors * n_op * width * width * wide
    sigma = pl.pallas_call(
        functools.partial(kernel, n_op, n_sec),
        out_shape=jax.ShapeDtypeStruct((sectors, rows, wide), jnp.bfloat16),
        in_specs=[
            pl.BlockSpec(memory_space=pltpu.SMEM),
            pl.BlockSpec(memory_space=pltpu.SMEM),
            pl.BlockSpec(memory_space=pl.ANY),
            pl.BlockSpec(memory_space=pl.ANY),
            pl.BlockSpec(memory_space=pl.ANY),
        ],
        out_specs=pl.BlockSpec(memory_space=pltpu.VMEM),
        scratch_shapes=[
            pltpu.VMEM((sectors, p_size, width, width), jnp.bfloat16),
            pltpu.VMEM((sectors, n_op, width, width), jnp.bfloat16),
            pltpu.VMEM((sectors, n_op, width, width), jnp.bfloat16),
            pltpu.VMEM((sectors, n_op, width, wide), jnp.bfloat16),
            pltpu.VMEM((sectors, width, wide), jnp.float32),
            pltpu.VMEM((sectors, width, wide), jnp.bfloat16),
            pltpu.VMEM((sectors, n_sec, rows, wide), jnp.bfloat16),
            pltpu.VMEM((sectors, rows, wide), jnp.bfloat16),
            pltpu.SemaphoreType.DMA((sectors,)),
            pltpu.SemaphoreType.DMA((sectors,)),
            pltpu.SemaphoreType.DMA((sectors,)),
            pltpu.SemaphoreType.DMA((sectors, n_sec, n_op)),
            pltpu.SemaphoreType.DMA((sectors, n_sec, n_op)),
            pltpu.SemaphoreType.DMA((sectors, n_sec)),
            pltpu.SemaphoreType.DMA((sectors, n_sec)),
            pltpu.SemaphoreType.DMA((sectors,)),
        ],
        compiler_params=pltpu.CompilerParams(
            collective_id=0, has_side_effects=True, vmem_limit_bytes=48 * MIB
        ),
        cost_estimate=pl.CostEstimate(flops=flops, bytes_accessed=12 * MIB, transcendentals=0),
    )(sites, sector_dims, waves, left, right)
    return sigma.reshape(sectors, rows, p_size, width)


def solution(mesh):
    placed = (
        P("op", None, None, None),
        P(),
        P(None, ("op", "sec"), None, None),
        P("op", None, "sec", None, None),
        P(),
    )
    return jax.shard_map(
        shards, mesh=mesh, in_specs=placed, out_specs=P("op", "sec", None, None), check_vma=False
    )
```

time: 72.5 us -> 71.6 us (0.988)
  other arithmetic: 3.34 us -> 0 us
  Pallas kernels: 66.5 us -> 68.3 us
  local copies, waits for them, and re-layouts: 2.07 us -> 3.14 us
    transpose x1 -> x0, other arithmetic: 2.13 us -> none  [shards(): masked = jnp.transpose(masked, (0, 2, 1, 3))]
    pallas_call x1, Pallas kernels: 66.5 us -> 68.3 us  [shards(): pl.pallas_call(functools.partial(kernel, n_op, n_sec), out_shape=jax.Shap...]
    convert_element_type x2 -> x0, other arithmetic: 1.21 us -> none  [the longest x1 1.14 us: shards(): (sigma * row_mask[:, :, None, None] * own_mask[:, None, None, :]).astype(...]
    unnamed x1 -> x5, local copies, waits for them, and re-layouts: 0.8 us -> 1.98 us
    reshape x0 -> x1, local copies, waits for them, and re-layouts: none -> 1.17 us  [shards(): return sigma.reshape(sectors, rows, p_size, width)]
    dynamic_slice x2 -> x0, local copies, waits for them, and re-layouts: 0.81 us -> none  [the longest x1 0.73 us: shards(): own_sizes = lax.dynamic_slice_in_dim(sector_dims, o * sectors, sectors)]
where the time goes in v2:
time: 71.6 us; the launch traced here: 71.5 us
  Pallas kernels  68.3 us (95%)
  local copies, waits for them, and re-layouts  3.14 us (4%)
    pallas_call x1, Pallas kernels, shards(): pl.pallas_call(functools.partial(kernel, n_op, n_sec), out_shape=jax.Shap...  68.3 us
    unnamed x5, local copies, waits for them, and re-layouts  1.98 us

profile of v2, /device:TPU:1, one launch (start us, length us, event | category | flops | bytes accessed | tf_op | source)
XLA Modules:
  0.0 71.5 jit_solution(1699271468337010618)
XLA Ops:
  0.0 0.0 copy-start
  0.0 0.0 copy-start.1
  0.0 2.0 %copy.8 = bf16[4,256,4,256]{3,1,2,0:T(8,128)(2,1)S(1)} copy(bf16[4,256,4,256]{3,2,1,0:T(4,128)(2,1)} %param.5) | data formatting | bytes 4194304 | tf_op args[0]
  2.0 0.0 copy-done
  2.0 0.0 copy-done.1
  2.0 68.3 %shard_map.55 = bf16[4,64,1024]{2,1,0:T(8,128)(2,1)S(1)} custom-call(f32[4,4,32]{2,1,0:T(4,128)S(1)} %bitcast.7, s32[32]{0:T(128)S(1)} %copy-done.1, bf16[4,4,256,256]{3,2,1,0:T(8,128)(2,1)S(1)} %bitcast.6, bf16[8,4,256,256]{3,2,1,0:T(8,128)(2,1)} %bitcast.8, bf16[4,8,256,256]{3,2,1,0:T(8,128)(2,1)} %bitcast.9), custom_call_target="tpu_custom_call" | custom-call | flops 8589934592 | bytes 12582912 | tf_op jit(solution)/shard_map/pallas_call | solution.py:253
  70.3 1.2 %reshape.11 = bf16[4,64,4,256]{3,2,1,0:T(4,128)(2,1)} reshape(bf16[4,64,1024]{2,1,0:T(8,128)(2,1)S(1)} %shard_map.55) | data formatting | bytes 1048576 | tf_op jit(solution)/shard_map/reshape | solution.py:287
Async XLA Ops:
  0.0 2.0 %copy-start = (f32[32,4,4]{0,2,1:T(4,128)S(1)}, f32[32,4,4]{0,2,1:T(4,128)}, u32[]{:S(2)}) copy-start(f32[32,4,4]{0,2,1:T(4,128)} %param.9) | copy-start | bytes 6148
  0.0 2.0 %copy-start.1 = (s32[32]{0:T(128)S(1)}, s32[32]{0:T(128)}, u32[]{:S(2)}) copy-start(s32[32]{0:T(128)} %dims_ref.1) | copy-start | bytes 388

commit v3 on v2

--- a/solution.py
+++ b/solution.py
@@ -9,6 +9,8 @@
 
 MESH = pl.DeviceIdType.MESH
 MIB = 1024 * 1024
+AHEAD = 3
+CHUNK = 64
 
 
 def kernel(
@@ -20,27 +22,16 @@
     z = lax.axis_index("sec")
     sectors, p_size, width = psi.shape[0], psi.shape[1], psi.shape[2]
     rows = width // n_sec
-    chunk = width // 4
+    tall = width // 2
+    per_half = n_sec // 2
     relays = n_sec == 4
 
-    if relays:
-        half = z // 2
-        beside = z + 1 - 2 * lax.rem(z, 2)
-        far = 3 * (1 - half)
-        order = [far, 2 - half, beside, z]
-        outer = lax.rem(z, 3) == 0
-    else:
-        order = [lax.rem(z + i, n_sec) for i in range(1, n_sec + 1)]
-
-    def units_of(j):
-        if j == sectors - 1:
-            parts = 4
-        elif j == 0:
-            parts = 2
-        else:
-            return [None]
-        each = n_sec // parts
-        return [order[i * each:(i + 1) * each] for i in range(parts)]
+    own_half = z // per_half
+    halves = [1 - own_half, own_half]
+    beside = z + 1 - 2 * lax.rem(z, 2)
+    far = 3 * halves[0]
+    near = 1 + halves[0]
+    outer = lax.rem(z, 3) == 0
 
     def psi_copy(j):
         return pltpu.make_async_copy(psi_hbm.at[j], psi.at[j], psi_sem.at[j])
@@ -52,16 +43,16 @@
         return pltpu.make_async_copy(left_hbm.at[o, j], left.at[j, o], own_sem.at[j])
 
     def rows_of(block):
-        if block is None:
-            return pl.ds(0, width)
         return pl.ds(pl.multiple_of(block * rows, rows), rows)
 
-    def left_copy(j, block, peer, slot):
-        which = 0 if block is None else block
+    def half_of(half):
+        return pl.ds(pl.multiple_of(half * tall, tall), tall)
+
+    def left_copy(j, half, peer, slot):
         return pltpu.make_async_remote_copy(
-            src_ref=left_hbm.at[peer, j, rows_of(block)],
-            dst_ref=left.at[j, slot, rows_of(block)],
-            send_sem=lsend_sem.at[j, which, peer], recv_sem=lrecv_sem.at[j, which, slot],
+            src_ref=left_hbm.at[peer, j, half_of(half)],
+            dst_ref=left.at[j, slot, half_of(half)],
+            send_sem=lsend_sem.at[j, half, peer], recv_sem=lrecv_sem.at[j, half, slot],
             device_id=(peer, z), device_id_type=MESH,
         )
 
@@ -91,8 +82,12 @@
             return 0
         lax.fori_loop(1, n_sec, step, 0)
 
-    def left_blocks(j):
-        return [block for unit in units_of(j) for block in (unit or [None])]
+    steps = [(j, half) for j in range(sectors) for half in halves]
+
+    def send_left(index):
+        if index < len(steps):
+            j, half = steps[index]
+            op_peers(lambda peer: left_copy(j, half, peer, o).start())
 
     barrier = pltpu.get_barrier_semaphore()
     op_peers(lambda peer: pl.semaphore_signal(
@@ -105,9 +100,8 @@
         own_copy(j).start()
     pl.semaphore_wait(barrier, n_op + n_sec - 2)
 
-    for j in range(sectors):
-        for block in left_blocks(j):
-            op_peers(lambda peer: left_copy(j, block, peer, o).start())
+    for index in range(AHEAD):
+        send_left(index)
 
     def mask_of(j, first, height):
         size = dims_ref[o * sectors + j]
@@ -126,30 +120,41 @@
             block = right[j, a]
             term = a * n_sec + z
             weights = [[site_ref[q, p, term] for p in range(p_size)] for q in range(p_size)]
-            for c in range(width // chunk):
-                here = pl.ds(c * chunk, chunk)
-                waves = psi[j, :, here, :].reshape(p_size * chunk, width)
-                got = lax.dot_general(
-                    waves, block, (((1,), (1,)), ((), ())), preferred_element_type=jnp.float32
-                )
+            got = lax.dot_general(
+                psi[j].reshape(p_size * width, width), block, (((1,), (1,)), ((), ())),
+                preferred_element_type=jnp.float32,
+            )
+            for c in range(width // CHUNK):
+                parts = [
+                    got[p * width + c * CHUNK:p * width + (c + 1) * CHUNK] for p in range(p_size)
+                ]
                 for q in range(p_size):
-                    value = weights[q][0] * got[:chunk]
+                    value = weights[q][0] * parts[0]
                     for p in range(1, p_size):
-                        value = value + weights[q][p] * got[p * chunk:(p + 1) * chunk]
-                    mixed[j, a, here, pl.ds(q * width, width)] = value.astype(jnp.bfloat16)
+                        value = value + weights[q][p] * parts[p]
+                    mixed[j, a, pl.ds(c * CHUNK, CHUNK), pl.ds(q * width, width)] = value.astype(
+                        jnp.bfloat16
+                    )
             return 0
 
         lax.fori_loop(0, n_op, one_term, 0)
 
-    def send_part(j, block):
-        if not relays:
-            part_copy(j, block, z).start()
-        elif block is far:
-            @pl.when(outer)
-            def _():
-                relay_copy(j).start()
+    def send_half(j, first):
+        if relays:
+            if first:
+                @pl.when(outer)
+                def _():
+                    relay_copy(j).start()
+
+                part_copy(j, near, z).start()
+            else:
+                part_copy(j, beside, z).start()
+        elif first:
+            for i in range(per_half):
+                part_copy(j, halves[0] * per_half + i, z).start()
         else:
-            part_copy(j, block, z).start()
+            for i in range(1, per_half):
+                part_copy(j, own_half * per_half + lax.rem(z + i, per_half), z).start()
 
     def relay(j):
         if not relays:
@@ -162,41 +167,32 @@
             zsend[j, rows_of(far), :] = value.astype(jnp.bfloat16)
             part_copy(j, far, z).start()
 
-    def contract(j, unit):
-        blocks = unit or [None]
-        for block in blocks:
-            op_peers(lambda peer: left_copy(j, block, peer, peer).wait_recv())
-
-        def left_rows(a):
-            parts = [left[j, a, rows_of(block), :] for block in blocks]
-            return parts[0] if len(parts) == 1 else jnp.concatenate(parts, axis=0)
+    def contract(index):
+        j, half = steps[index]
+        op_peers(lambda peer: left_copy(j, half, peer, peer).wait_recv())
+        op_peers(lambda peer: left_copy(j, half, peer, o).wait_send())
+        send_left(index + AHEAD)
+        here = half_of(half)
 
         def one_state(q, _):
             cols = pl.ds(pl.multiple_of(q * width, width), width)
             value = jnp.dot(
-                left_rows(0), mixed[j, 0, :, cols], preferred_element_type=jnp.float32
+                jnp.concatenate([left[j, a, here, :] for a in range(n_op)], axis=1),
+                mixed[j, :, :, cols].reshape(n_op * width, width),
+                preferred_element_type=jnp.float32,
             )
-            for a in range(1, n_op):
-                value = value + jnp.dot(
-                    left_rows(a), mixed[j, a, :, cols], preferred_element_type=jnp.float32
-                )
-            height = value.shape[0] // len(blocks)
-            for i, block in enumerate(blocks):
-                part = value[i * height:(i + 1) * height]
-                total[j, rows_of(block), cols] = part
-                zsend[j, rows_of(block), cols] = part.astype(jnp.bfloat16)
+            total[j, here, cols] = value
+            zsend[j, here, cols] = value.astype(jnp.bfloat16)
             return 0
 
         lax.fori_loop(0, p_size, one_state, 0)
-        for block in (unit or order):
-            if block is not order[-1]:
-                send_part(j, block)
+        send_half(j, index % 2 == 0)
 
     def finish(j):
         own = rows_of(z)
         inside = mask_of(j, z * rows, rows)
         if relays:
-            part_copy(j, 2 - half, 2 - half).wait_recv()
+            part_copy(j, near, near).wait_recv()
             part_copy(j, beside, beside).wait_recv()
 
             @pl.when(jnp.logical_not(outer))
@@ -204,10 +200,10 @@
                 part_copy(j, far, far).wait_recv()
                 total[j, own, :] = total[j, own, :] + zrecv[j, far].astype(jnp.float32)
 
-            peers = [2 - half, beside]
+            peers = [near, beside]
         else:
             sec_peers(lambda peer: part_copy(j, peer, peer).wait_recv())
-            peers = order[:-1]
+            peers = [lax.rem(z + i, n_sec) for i in range(1, n_sec)]
         for q in range(p_size):
             cols = pl.ds(q * width, width)
             value = total[j, own, cols]
@@ -224,18 +220,16 @@
             for i in range(last - 1):
                 finish(i)
         own_copy(j).wait()
-        for i, unit in enumerate(units_of(j)):
-            contract(j, unit)
-            if i == 0 and j > 0:
-                relay(j - 1)
-            if i == 1 and j == last:
-                relay(j)
+        contract(2 * j)
+        if j > 0:
+            relay(j - 1)
+        if j == last:
+            relay(j)
+        contract(2 * j + 1)
     for j in range(max(last - 1, 0), sectors):
         finish(j)
 
     for j in range(sectors):
-        for block in left_blocks(j):
-            op_peers(lambda peer: left_copy(j, block, peer, o).wait_send())
         sec_peers(lambda peer: part_copy(j, peer, z).wait_send())
 
 
@@ -273,8 +267,8 @@
             pltpu.SemaphoreType.DMA((sectors,)),
             pltpu.SemaphoreType.DMA((sectors,)),
             pltpu.SemaphoreType.DMA((sectors,)),
-            pltpu.SemaphoreType.DMA((sectors, n_sec, n_op)),
-            pltpu.SemaphoreType.DMA((sectors, n_sec, n_op)),
+            pltpu.SemaphoreType.DMA((sectors, 2, n_op)),
+            pltpu.SemaphoreType.DMA((sectors, 2, n_op)),
             pltpu.SemaphoreType.DMA((sectors, n_sec)),
             pltpu.SemaphoreType.DMA((sectors, n_sec)),
             pltpu.SemaphoreType.DMA((sectors,)),

time: 71.6 us -> 68.3 us (0.954)
  Pallas kernels: 68.3 us -> 65 us
    pallas_call x1, Pallas kernels: 68.3 us -> 65 us  [shards(): pl.pallas_call(functools.partial(kernel, n_op, n_sec), out_shape=jax.Shap...]
where the time goes in v3:
time: 68.3 us; the launch traced here: 68.1 us
  Pallas kernels  65 us (95%)
  local copies, waits for them, and re-layouts  3.14 us (5%)
    pallas_call x1, Pallas kernels, shards(): pl.pallas_call(functools.partial(kernel, n_op, n_sec), out_shape=jax.Shap...  65 us
    unnamed x5, local copies, waits for them, and re-layouts  1.98 us

profile of v3, /device:TPU:1, one launch (start us, length us, event | category | flops | bytes accessed | tf_op | source)
XLA Modules:
  0.0 68.1 jit_solution(8726561637313485577)
XLA Ops:
  0.0 0.0 copy-start
  0.0 0.0 copy-start.1
  0.0 2.0 %copy.8 = bf16[4,256,4,256]{3,1,2,0:T(8,128)(2,1)S(1)} copy(bf16[4,256,4,256]{3,2,1,0:T(4,128)(2,1)} %param.5) | data formatting | bytes 4194304 | tf_op args[0]
  2.0 0.0 copy-done
  2.0 0.0 copy-done.1
  2.0 65.0 %shard_map.55 = bf16[4,64,1024]{2,1,0:T(8,128)(2,1)S(1)} custom-call(f32[4,4,32]{2,1,0:T(4,128)S(1)} %bitcast.7, s32[32]{0:T(128)S(1)} %copy-done.1, bf16[4,4,256,256]{3,2,1,0:T(8,128)(2,1)S(1)} %bitcast.6, bf16[8,4,256,256]{3,2,1,0:T(8,128)(2,1)} %bitcast.8, bf16[4,8,256,256]{3,2,1,0:T(8,128)(2,1)} %bitcast.9), custom_call_target="tpu_custom_call" | custom-call | flops 8589934592 | bytes 12582912 | tf_op jit(solution)/shard_map/pallas_call | solution.py:247
  67.0 1.2 %reshape.11 = bf16[4,64,4,256]{3,2,1,0:T(4,128)(2,1)} reshape(bf16[4,64,1024]{2,1,0:T(8,128)(2,1)S(1)} %shard_map.55) | data formatting | bytes 1048576 | tf_op jit(solution)/shard_map/reshape | solution.py:281
Async XLA Ops:
  0.0 2.0 %copy-start = (f32[32,4,4]{0,2,1:T(4,128)S(1)}, f32[32,4,4]{0,2,1:T(4,128)}, u32[]{:S(2)}) copy-start(f32[32,4,4]{0,2,1:T(4,128)} %param.9) | copy-start | bytes 6148
  0.0 2.0 %copy-start.1 = (s32[32]{0:T(128)S(1)}, s32[32]{0:T(128)}, u32[]{:S(2)}) copy-start(s32[32]{0:T(128)} %dims_ref.1) | copy-start | bytes 388

commit v4 on v3

--- a/solution.py
+++ b/solution.py
@@ -9,14 +9,14 @@
 
 MESH = pl.DeviceIdType.MESH
 MIB = 1024 * 1024
-AHEAD = 3
+AHEAD = 4
 CHUNK = 64
 
 
 def kernel(
-    n_op, n_sec, site_ref, dims_ref, psi_hbm, left_hbm, right_hbm, out_ref,
-    psi, right, left, mixed, total, zsend, zrecv, relayed,
-    psi_sem, right_sem, own_sem, lsend_sem, lrecv_sem, zsend_sem, zrecv_sem, relay_sem,
+    n_op, n_sec, site_ref, dims_ref, wave_hbm, left_hbm, right_hbm, out_ref,
+    wave, psi, right, left, mixed, total, zsend, zrecv, relayed,
+    wave_sem, right_sem, own_sem, lsend_sem, lrecv_sem, zsend_sem, zrecv_sem, relay_sem,
 ):
     o = lax.axis_index("op")
     z = lax.axis_index("sec")
@@ -33,8 +33,8 @@
     near = 1 + halves[0]
     outer = lax.rem(z, 3) == 0
 
-    def psi_copy(j):
-        return pltpu.make_async_copy(psi_hbm.at[j], psi.at[j], psi_sem.at[j])
+    def wave_copy(j):
+        return pltpu.make_async_copy(wave_hbm.at[j], wave.at[j], wave_sem.at[j])
 
     def right_copy(j):
         return pltpu.make_async_copy(right_hbm.at[j], right.at[j], right_sem.at[j])
@@ -45,14 +45,13 @@
     def rows_of(block):
         return pl.ds(pl.multiple_of(block * rows, rows), rows)
 
-    def half_of(half):
-        return pl.ds(pl.multiple_of(half * tall, tall), tall)
-
-    def left_copy(j, half, peer, slot):
+    def left_copy(step, peer, slot):
+        j, piece, first, height, _ = step
+        here = pl.ds(pl.multiple_of(first, height), height)
         return pltpu.make_async_remote_copy(
-            src_ref=left_hbm.at[peer, j, half_of(half)],
-            dst_ref=left.at[j, slot, half_of(half)],
-            send_sem=lsend_sem.at[j, half, peer], recv_sem=lrecv_sem.at[j, half, slot],
+            src_ref=left_hbm.at[peer, j, here],
+            dst_ref=left.at[j, slot, here],
+            send_sem=lsend_sem.at[j, piece, peer], recv_sem=lrecv_sem.at[j, piece, slot],
             device_id=(peer, z), device_id_type=MESH,
         )
 
@@ -82,12 +81,18 @@
             return 0
         lax.fori_loop(1, n_sec, step, 0)
 
-    steps = [(j, half) for j in range(sectors) for half in halves]
+    steps = []
+    for j in range(sectors):
+        steps.append((j, 0, halves[0] * tall, tall, "other"))
+        if relays and j == sectors - 1:
+            steps.append((j, 1, beside * rows, rows, "beside"))
+            steps.append((j, 2, z * rows, rows, "none"))
+        else:
+            steps.append((j, 1, halves[1] * tall, tall, "beside"))
 
     def send_left(index):
         if index < len(steps):
-            j, half = steps[index]
-            op_peers(lambda peer: left_copy(j, half, peer, o).start())
+            op_peers(lambda peer: left_copy(steps[index], peer, o).start())
 
     barrier = pltpu.get_barrier_semaphore()
     op_peers(lambda peer: pl.semaphore_signal(
@@ -95,7 +100,7 @@
     sec_peers(lambda peer: pl.semaphore_signal(
         barrier, inc=1, device_id=(o, peer), device_id_type=MESH))
     for j in range(sectors):
-        psi_copy(j).start()
+        wave_copy(j).start()
         right_copy(j).start()
         own_copy(j).start()
     pl.semaphore_wait(barrier, n_op + n_sec - 2)
@@ -110,11 +115,16 @@
         return jnp.where((down < size) & (across < size), 1.0, 0.0).astype(jnp.float32)
 
     def mix(j):
-        psi_copy(j).wait()
+        wave_copy(j).wait()
         right_copy(j).wait()
-        inside = mask_of(j, 0, width).astype(jnp.bfloat16)
-        for p in range(p_size):
-            psi[j, p] = psi[j, p] * inside
+
+        def lay_out(c, _):
+            here = pl.ds(pl.multiple_of(c * CHUNK, CHUNK), CHUNK)
+            inside = mask_of(j, c * CHUNK, CHUNK).astype(jnp.bfloat16)
+            psi[j, :, here, :] = jnp.swapaxes(wave[j, here], 0, 1) * inside[None]
+            return 0
+
+        lax.fori_loop(0, width // CHUNK, lay_out, 0)
 
         def one_term(a, _):
             block = right[j, a]
@@ -139,9 +149,11 @@
 
         lax.fori_loop(0, n_op, one_term, 0)
 
-    def send_half(j, first):
+    def send_parts(j, which):
+        if which == "none":
+            return
         if relays:
-            if first:
+            if which == "other":
                 @pl.when(outer)
                 def _():
                     relay_copy(j).start()
@@ -149,7 +161,7 @@
                 part_copy(j, near, z).start()
             else:
                 part_copy(j, beside, z).start()
-        elif first:
+        elif which == "other":
             for i in range(per_half):
                 part_copy(j, halves[0] * per_half + i, z).start()
         else:
@@ -168,11 +180,12 @@
             part_copy(j, far, z).start()
 
     def contract(index):
-        j, half = steps[index]
-        op_peers(lambda peer: left_copy(j, half, peer, peer).wait_recv())
-        op_peers(lambda peer: left_copy(j, half, peer, o).wait_send())
+        step = steps[index]
+        j, _, first, height, which = step
+        op_peers(lambda peer: left_copy(step, peer, peer).wait_recv())
+        op_peers(lambda peer: left_copy(step, peer, o).wait_send())
         send_left(index + AHEAD)
-        here = half_of(half)
+        here = pl.ds(pl.multiple_of(first, height), height)
 
         def one_state(q, _):
             cols = pl.ds(pl.multiple_of(q * width, width), width)
@@ -186,7 +199,7 @@
             return 0
 
         lax.fori_loop(0, p_size, one_state, 0)
-        send_half(j, index % 2 == 0)
+        send_parts(j, which)
 
     def finish(j):
         own = rows_of(z)
@@ -204,12 +217,14 @@
         else:
             sec_peers(lambda peer: part_copy(j, peer, peer).wait_recv())
             peers = [lax.rem(z + i, n_sec) for i in range(1, n_sec)]
+        states = []
         for q in range(p_size):
             cols = pl.ds(q * width, width)
             value = total[j, own, cols]
             for peer in peers:
                 value = value + zrecv[j, peer, :, cols].astype(jnp.float32)
-            out_ref[j, :, cols] = (value * inside).astype(jnp.bfloat16)
+            states.append((value * inside).astype(jnp.bfloat16))
+        out_ref[j] = jnp.swapaxes(jnp.stack(states), 0, 1)
 
     mix(0)
     last = sectors - 1
@@ -226,8 +241,11 @@
         if j == last:
             relay(j)
         contract(2 * j + 1)
-    for j in range(max(last - 1, 0), sectors):
-        finish(j)
+    if last > 0:
+        finish(last - 1)
+    if relays:
+        contract(2 * sectors)
+    finish(last)
 
     for j in range(sectors):
         sec_peers(lambda peer: part_copy(j, peer, z).wait_send())
@@ -238,15 +256,14 @@
     n_sec = lax.axis_size("sec")
     sectors, width, p_size = wave.shape[0], wave.shape[1], wave.shape[2]
     rows = width // n_sec
-    waves = jnp.transpose(wave, (0, 2, 1, 3))
     left = left_ops.reshape(n_op, sectors, width, width)
     right = right_ops.reshape(sectors, n_op, width, width)
     sites = jnp.transpose(site_ops, (1, 2, 0))
     wide = p_size * width
     flops = 4 * sectors * n_op * width * width * wide
-    sigma = pl.pallas_call(
+    return pl.pallas_call(
         functools.partial(kernel, n_op, n_sec),
-        out_shape=jax.ShapeDtypeStruct((sectors, rows, wide), jnp.bfloat16),
+        out_shape=jax.ShapeDtypeStruct((sectors, rows, p_size, width), jnp.bfloat16),
         in_specs=[
             pl.BlockSpec(memory_space=pltpu.SMEM),
             pl.BlockSpec(memory_space=pltpu.SMEM),
@@ -256,6 +273,7 @@
         ],
         out_specs=pl.BlockSpec(memory_space=pltpu.VMEM),
         scratch_shapes=[
+            pltpu.VMEM((sectors, width, p_size, width), jnp.bfloat16),
             pltpu.VMEM((sectors, p_size, width, width), jnp.bfloat16),
             pltpu.VMEM((sectors, n_op, width, width), jnp.bfloat16),
             pltpu.VMEM((sectors, n_op, width, width), jnp.bfloat16),
@@ -267,18 +285,17 @@
             pltpu.SemaphoreType.DMA((sectors,)),
             pltpu.SemaphoreType.DMA((sectors,)),
             pltpu.SemaphoreType.DMA((sectors,)),
-            pltpu.SemaphoreType.DMA((sectors, 2, n_op)),
-            pltpu.SemaphoreType.DMA((sectors, 2, n_op)),
+            pltpu.SemaphoreType.DMA((sectors, 3, n_op)),
+            pltpu.SemaphoreType.DMA((sectors, 3, n_op)),
             pltpu.SemaphoreType.DMA((sectors, n_sec)),
             pltpu.SemaphoreType.DMA((sectors, n_sec)),
             pltpu.SemaphoreType.DMA((sectors,)),
         ],
         compiler_params=pltpu.CompilerParams(
-            collective_id=0, has_side_effects=True, vmem_limit_bytes=48 * MIB
+            collective_id=0, has_side_effects=True, vmem_limit_bytes=56 * MIB
         ),
         cost_estimate=pl.CostEstimate(flops=flops, bytes_accessed=12 * MIB, transcendentals=0),
-    )(sites, sector_dims, waves, left, right)
-    return sigma.reshape(sectors, rows, p_size, width)
+    )(sites, sector_dims, wave, left, right)
 
 
 def solution(mesh):

time: 68.3 us -> 68.8 us (level)
  Pallas kernels: 65 us -> 66.4 us
  local copies, waits for them, and re-layouts: 3.14 us -> 2.02 us
    pallas_call x1, Pallas kernels: 65 us -> 66.4 us  [shards(): pl.pallas_call(functools.partial(kernel, n_op, n_sec), out_shape=jax.Shap...]
    reshape x1 -> x0, local copies, waits for them, and re-layouts: 1.17 us -> none  [shards(): return sigma.reshape(sectors, rows, p_size, width)]
    unnamed x5 -> x1, local copies, waits for them, and re-layouts: 1.98 us -> 2.02 us
where the time goes in v4:
time: 68.8 us; the launch traced here: 68.4 us
  Pallas kernels  66.4 us (97%)
  local copies, waits for them, and re-layouts  2.02 us (3%)
    pallas_call x1, Pallas kernels, shards(): pl.pallas_call(functools.partial(kernel, n_op, n_sec), out_shape=jax.Shap...  66.4 us
    unnamed x1, local copies, waits for them, and re-layouts  2.02 us

profile of v4, /device:TPU:1, one launch (start us, length us, event | category | flops | bytes accessed | tf_op | source)
XLA Modules:
  0.0 68.4 jit_solution(6551903462742601714)
XLA Ops:
  0.0 66.4 %shard_map.55 = bf16[4,64,4,256]{3,2,1,0:T(4,128)(2,1)} custom-call(f32[4,4,32]{2,1,0:T(4,128)} %bitcast.5, s32[32]{0:T(128)} %dims_ref.1, bf16[4,256,4,256]{3,2,1,0:T(4,128)(2,1)} %wave_hbm.1, bf16[8,4,256,256]{3,2,1,0:T(8,128)(2,1)} %bitcast.3, bf16[4,8,256,256]{3,2,1,0:T(8,128)(2,1)} %bitcast.4), custom_call_target="tpu_custom_call" | custom-call | flops 8589934592 | bytes 12582912 | tf_op jit(solution)/shard_map/pallas_call | solution.py:264
  66.4 2.0 %copy.7 = bf16[4,64,4,256]{3,2,1,0:T(4,128)(2,1)} copy(bf16[4,64,4,256]{3,2,1,0:T(4,128)(2,1)} %shard_map.55) | data formatting | bytes 1048576

commit v5 on v4

--- a/solution.py
+++ b/solution.py
@@ -20,7 +20,8 @@
 ):
     o = lax.axis_index("op")
     z = lax.axis_index("sec")
-    sectors, p_size, width = psi.shape[0], psi.shape[1], psi.shape[2]
+    sectors, width, p_size = wave.shape[0], wave.shape[1], wave.shape[2]
+    chunks = width // CHUNK
     rows = width // n_sec
     tall = width // 2
     per_half = n_sec // 2
@@ -46,7 +47,7 @@
         return pl.ds(pl.multiple_of(block * rows, rows), rows)
 
     def left_copy(step, peer, slot):
-        j, piece, first, height, _ = step
+        j, piece, first, height = step
         here = pl.ds(pl.multiple_of(first, height), height)
         return pltpu.make_async_remote_copy(
             src_ref=left_hbm.at[peer, j, here],
@@ -83,12 +84,12 @@
 
     steps = []
     for j in range(sectors):
-        steps.append((j, 0, halves[0] * tall, tall, "other"))
+        steps.append((j, 0, halves[0] * tall, tall))
         if relays and j == sectors - 1:
-            steps.append((j, 1, beside * rows, rows, "beside"))
-            steps.append((j, 2, z * rows, rows, "none"))
+            steps.append((j, 1, beside * rows, rows))
+            steps.append((j, 2, z * rows, rows))
         else:
-            steps.append((j, 1, halves[1] * tall, tall, "beside"))
+            steps.append((j, 1, halves[1] * tall, tall))
 
     def send_left(index):
         if index < len(steps):
@@ -121,10 +122,10 @@
         def lay_out(c, _):
             here = pl.ds(pl.multiple_of(c * CHUNK, CHUNK), CHUNK)
             inside = mask_of(j, c * CHUNK, CHUNK).astype(jnp.bfloat16)
-            psi[j, :, here, :] = jnp.swapaxes(wave[j, here], 0, 1) * inside[None]
-            return 0
-
-        lax.fori_loop(0, width // CHUNK, lay_out, 0)
+            psi[j, c] = jnp.swapaxes(wave[j, here], 0, 1) * inside[None]
+            return 0
+
+        lax.fori_loop(0, chunks, lay_out, 0)
 
         def one_term(a, _):
             block = right[j, a]
@@ -134,9 +135,10 @@
                 psi[j].reshape(p_size * width, width), block, (((1,), (1,)), ((), ())),
                 preferred_element_type=jnp.float32,
             )
-            for c in range(width // CHUNK):
+            for c in range(chunks):
                 parts = [
-                    got[p * width + c * CHUNK:p * width + (c + 1) * CHUNK] for p in range(p_size)
+                    got[(c * p_size + p) * CHUNK:(c * p_size + p + 1) * CHUNK]
+                    for p in range(p_size)
                 ]
                 for q in range(p_size):
                     value = weights[q][0] * parts[0]
@@ -147,11 +149,9 @@
                     )
             return 0
 
-        lax.fori_loop(0, n_op, one_term, 0)
+        lax.fori_loop(0, n_op, one_term, 0, unroll=2)
 
     def send_parts(j, which):
-        if which == "none":
-            return
         if relays:
             if which == "other":
                 @pl.when(outer)
@@ -179,12 +179,11 @@
             zsend[j, rows_of(far), :] = value.astype(jnp.bfloat16)
             part_copy(j, far, z).start()
 
-    def contract(index):
-        step = steps[index]
-        j, _, first, height, which = step
-        op_peers(lambda peer: left_copy(step, peer, peer).wait_recv())
-        op_peers(lambda peer: left_copy(step, peer, o).wait_send())
-        send_left(index + AHEAD)
+    def contract(indices, j, first, height, which):
+        for index in indices:
+            op_peers(lambda peer: left_copy(steps[index], peer, peer).wait_recv())
+            op_peers(lambda peer: left_copy(steps[index], peer, o).wait_send())
+            send_left(index + AHEAD)
         here = pl.ds(pl.multiple_of(first, height), height)
 
         def one_state(q, _):
@@ -198,8 +197,9 @@
             zsend[j, here, cols] = value.astype(jnp.bfloat16)
             return 0
 
-        lax.fori_loop(0, p_size, one_state, 0)
-        send_parts(j, which)
+        lax.fori_loop(0, p_size, one_state, 0, unroll=2)
+        for part in which:
+            send_parts(j, part)
 
     def finish(j):
         own = rows_of(z)
@@ -217,14 +217,12 @@
         else:
             sec_peers(lambda peer: part_copy(j, peer, peer).wait_recv())
             peers = [lax.rem(z + i, n_sec) for i in range(1, n_sec)]
-        states = []
         for q in range(p_size):
             cols = pl.ds(q * width, width)
             value = total[j, own, cols]
             for peer in peers:
                 value = value + zrecv[j, peer, :, cols].astype(jnp.float32)
-            states.append((value * inside).astype(jnp.bfloat16))
-        out_ref[j] = jnp.swapaxes(jnp.stack(states), 0, 1)
+            out_ref[j, :, cols] = (value * inside).astype(jnp.bfloat16)
 
     mix(0)
     last = sectors - 1
@@ -235,16 +233,23 @@
             for i in range(last - 1):
                 finish(i)
         own_copy(j).wait()
-        contract(2 * j)
-        if j > 0:
-            relay(j - 1)
-        if j == last:
+        if j < last:
+            contract([2 * j, 2 * j + 1], j, 0, width, ["other", "beside"])
+            if j > 0:
+                relay(j - 1)
+        else:
+            contract([2 * j], j, halves[0] * tall, tall, ["other"])
+            if j > 0:
+                relay(j - 1)
             relay(j)
-        contract(2 * j + 1)
+    if relays:
+        contract([2 * last + 1], last, beside * rows, rows, ["beside"])
+    else:
+        contract([2 * last + 1], last, halves[1] * tall, tall, ["beside"])
     if last > 0:
         finish(last - 1)
     if relays:
-        contract(2 * sectors)
+        contract([2 * last + 2], last, z * rows, rows, [])
     finish(last)
 
     for j in range(sectors):
@@ -261,9 +266,9 @@
     sites = jnp.transpose(site_ops, (1, 2, 0))
     wide = p_size * width
     flops = 4 * sectors * n_op * width * width * wide
-    return pl.pallas_call(
+    sigma = pl.pallas_call(
         functools.partial(kernel, n_op, n_sec),
-        out_shape=jax.ShapeDtypeStruct((sectors, rows, p_size, width), jnp.bfloat16),
+        out_shape=jax.ShapeDtypeStruct((sectors, rows, wide), jnp.bfloat16),
         in_specs=[
             pl.BlockSpec(memory_space=pltpu.SMEM),
             pl.BlockSpec(memory_space=pltpu.SMEM),
@@ -274,7 +279,7 @@
         out_specs=pl.BlockSpec(memory_space=pltpu.VMEM),
         scratch_shapes=[
             pltpu.VMEM((sectors, width, p_size, width), jnp.bfloat16),
-            pltpu.VMEM((sectors, p_size, width, width), jnp.bfloat16),
+            pltpu.VMEM((sectors, width // CHUNK, p_size, CHUNK, width), jnp.bfloat16),
             pltpu.VMEM((sectors, n_op, width, width), jnp.bfloat16),
             pltpu.VMEM((sectors, n_op, width, width), jnp.bfloat16),
             pltpu.VMEM((sectors, n_op, width, wide), jnp.bfloat16),
@@ -296,6 +301,7 @@
         ),
         cost_estimate=pl.CostEstimate(flops=flops, bytes_accessed=12 * MIB, transcendentals=0),
     )(sites, sector_dims, wave, left, right)
+    return sigma.reshape(sectors, rows, p_size, width)
 
 
 def solution(mesh):

time: 68.8 us -> 72.8 us (1.058); the launches traced: 68.4 us -> 71.5 us
  Pallas kernels: 66.4 us -> 69.3 us
    pallas_call x1, Pallas kernels: 66.4 us -> 69.3 us  [shards(): pl.pallas_call(functools.partial(kernel, n_op, n_sec), out_shape=jax.Shap...]
    reshape x0 -> x1, local copies, waits for them, and re-layouts: none -> 2.23 us  [shards(): return sigma.reshape(sectors, rows, p_size, width)]
    unnamed x1 -> x0, local copies, waits for them, and re-layouts: 2.02 us -> none
where the time goes in v5:
time: 72.8 us; the launch traced here: 71.5 us
  Pallas kernels  69.3 us (95%)
  local copies, waits for them, and re-layouts  2.23 us (3%)
    pallas_call x1, Pallas kernels, shards(): pl.pallas_call(functools.partial(kernel, n_op, n_sec), out_shape=jax.Shap...  69.3 us
    reshape x1, local copies, waits for them, and re-layouts, shards(): return sigma.reshape(sectors, rows, p_size, width)  2.23 us

profile of v5, /device:TPU:1, one launch (start us, length us, event | category | flops | bytes accessed | tf_op | source)
XLA Modules:
  0.0 71.5 jit_solution(2722937010330992909)
XLA Ops:
  0.0 69.3 %shard_map.55 = bf16[4,64,1024]{2,1,0:T(8,128)(2,1)} custom-call(f32[4,4,32]{2,1,0:T(4,128)} %bitcast.5, s32[32]{0:T(128)} %dims_ref.1, bf16[4,256,4,256]{3,2,1,0:T(4,128)(2,1)} %wave_hbm.1, bf16[8,4,256,256]{3,2,1,0:T(8,128)(2,1)} %bitcast.3, bf16[4,8,256,256]{3,2,1,0:T(8,128)(2,1)} %bitcast.4), custom_call_target="tpu_custom_call" | custom-call | flops 8589934592 | bytes 12582912 | tf_op jit(solution)/shard_map/pallas_call | solution.py:269
  69.3 2.2 %reshape.11 = bf16[4,64,4,256]{3,2,1,0:T(4,128)(2,1)} reshape(bf16[4,64,1024]{2,1,0:T(8,128)(2,1)} %shard_map.55) | data formatting | bytes 1048576 | tf_op jit(solution)/shard_map/reshape | solution.py:304

commit v6 on v3

--- a/solution.py
+++ b/solution.py
@@ -9,14 +9,14 @@
 
 MESH = pl.DeviceIdType.MESH
 MIB = 1024 * 1024
-AHEAD = 3
+AHEAD = 4
 CHUNK = 64
 
 
 def kernel(
     n_op, n_sec, site_ref, dims_ref, psi_hbm, left_hbm, right_hbm, out_ref,
     psi, right, left, mixed, total, zsend, zrecv, relayed,
-    psi_sem, right_sem, own_sem, lsend_sem, lrecv_sem, zsend_sem, zrecv_sem, relay_sem,
+    psi_sem, right_sem, lsend_sem, lrecv_sem, zsend_sem, zrecv_sem, relay_sem,
 ):
     o = lax.axis_index("op")
     z = lax.axis_index("sec")
@@ -39,22 +39,34 @@
     def right_copy(j):
         return pltpu.make_async_copy(right_hbm.at[j], right.at[j], right_sem.at[j])
 
-    def own_copy(j):
-        return pltpu.make_async_copy(left_hbm.at[o, j], left.at[j, o], own_sem.at[j])
-
     def rows_of(block):
         return pl.ds(pl.multiple_of(block * rows, rows), rows)
 
-    def half_of(half):
-        return pl.ds(pl.multiple_of(half * tall, tall), tall)
-
-    def left_copy(j, half, peer, slot):
+    def rows_in(step):
+        return pl.ds(pl.multiple_of(step[2], step[3]), step[3])
+
+    def left_copy(step, peer):
+        j, piece = step[:2]
         return pltpu.make_async_remote_copy(
-            src_ref=left_hbm.at[peer, j, half_of(half)],
-            dst_ref=left.at[j, slot, half_of(half)],
-            send_sem=lsend_sem.at[j, half, peer], recv_sem=lrecv_sem.at[j, half, slot],
+            src_ref=left_hbm.at[peer, j, rows_in(step)],
+            dst_ref=left.at[j, o, rows_in(step)],
+            send_sem=lsend_sem.at[j, piece], recv_sem=lrecv_sem.at[j, piece],
             device_id=(peer, z), device_id_type=MESH,
         )
+
+    def own_copy(step):
+        j, piece = step[:2]
+        return pltpu.make_async_copy(
+            left_hbm.at[o, j, rows_in(step)], left.at[j, o, rows_in(step)],
+            lrecv_sem.at[j, piece],
+        )
+
+    def wait_left(step):
+        j, piece = step[:2]
+        came = left.at[j, :, rows_in(step)]
+        pltpu.make_async_copy(came, came, lrecv_sem.at[j, piece]).wait()
+        gone = left.at[j, pl.ds(0, n_op - 1), rows_in(step)]
+        pltpu.make_async_copy(gone, gone, lsend_sem.at[j, piece]).wait()
 
     def part_copy(j, peer, slot):
         return pltpu.make_async_remote_copy(
@@ -82,12 +94,19 @@
             return 0
         lax.fori_loop(1, n_sec, step, 0)
 
-    steps = [(j, half) for j in range(sectors) for half in halves]
+    steps = []
+    for j in range(sectors):
+        steps.append((j, 0, halves[0] * tall, tall, "other"))
+        if relays and j == sectors - 1:
+            steps.append((j, 1, beside * rows, rows, "beside"))
+            steps.append((j, 2, z * rows, rows, "none"))
+        else:
+            steps.append((j, 1, halves[1] * tall, tall, "beside"))
 
     def send_left(index):
         if index < len(steps):
-            j, half = steps[index]
-            op_peers(lambda peer: left_copy(j, half, peer, o).start())
+            op_peers(lambda peer: left_copy(steps[index], peer).start())
+            own_copy(steps[index]).start()
 
     barrier = pltpu.get_barrier_semaphore()
     op_peers(lambda peer: pl.semaphore_signal(
@@ -97,7 +116,6 @@
     for j in range(sectors):
         psi_copy(j).start()
         right_copy(j).start()
-        own_copy(j).start()
     pl.semaphore_wait(barrier, n_op + n_sec - 2)
 
     for index in range(AHEAD):
@@ -139,9 +157,11 @@
 
         lax.fori_loop(0, n_op, one_term, 0)
 
-    def send_half(j, first):
+    def send_parts(j, which):
+        if which == "none":
+            return
         if relays:
-            if first:
+            if which == "other":
                 @pl.when(outer)
                 def _():
                     relay_copy(j).start()
@@ -149,7 +169,7 @@
                 part_copy(j, near, z).start()
             else:
                 part_copy(j, beside, z).start()
-        elif first:
+        elif which == "other":
             for i in range(per_half):
                 part_copy(j, halves[0] * per_half + i, z).start()
         else:
@@ -168,11 +188,11 @@
             part_copy(j, far, z).start()
 
     def contract(index):
-        j, half = steps[index]
-        op_peers(lambda peer: left_copy(j, half, peer, peer).wait_recv())
-        op_peers(lambda peer: left_copy(j, half, peer, o).wait_send())
+        step = steps[index]
+        j, which = step[0], step[4]
+        wait_left(step)
         send_left(index + AHEAD)
-        here = half_of(half)
+        here = rows_in(step)
 
         def one_state(q, _):
             cols = pl.ds(pl.multiple_of(q * width, width), width)
@@ -186,7 +206,7 @@
             return 0
 
         lax.fori_loop(0, p_size, one_state, 0)
-        send_half(j, index % 2 == 0)
+        send_parts(j, which)
 
     def finish(j):
         own = rows_of(z)
@@ -219,15 +239,17 @@
         if j == last:
             for i in range(last - 1):
                 finish(i)
-        own_copy(j).wait()
         contract(2 * j)
         if j > 0:
             relay(j - 1)
         if j == last:
             relay(j)
         contract(2 * j + 1)
-    for j in range(max(last - 1, 0), sectors):
-        finish(j)
+    if last > 0:
+        finish(last - 1)
+    if relays:
+        contract(2 * sectors)
+    finish(last)
 
     for j in range(sectors):
         sec_peers(lambda peer: part_copy(j, peer, z).wait_send())
@@ -238,12 +260,12 @@
     n_sec = lax.axis_size("sec")
     sectors, width, p_size = wave.shape[0], wave.shape[1], wave.shape[2]
     rows = width // n_sec
-    waves = jnp.transpose(wave, (0, 2, 1, 3))
     left = left_ops.reshape(n_op, sectors, width, width)
     right = right_ops.reshape(sectors, n_op, width, width)
     sites = jnp.transpose(site_ops, (1, 2, 0))
     wide = p_size * width
     flops = 4 * sectors * n_op * width * width * wide
+    waves = jnp.transpose(wave, (0, 2, 1, 3))
     sigma = pl.pallas_call(
         functools.partial(kernel, n_op, n_sec),
         out_shape=jax.ShapeDtypeStruct((sectors, rows, wide), jnp.bfloat16),
@@ -266,9 +288,8 @@
             pltpu.VMEM((sectors, rows, wide), jnp.bfloat16),
             pltpu.SemaphoreType.DMA((sectors,)),
             pltpu.SemaphoreType.DMA((sectors,)),
-            pltpu.SemaphoreType.DMA((sectors,)),
-            pltpu.SemaphoreType.DMA((sectors, 2, n_op)),
-            pltpu.SemaphoreType.DMA((sectors, 2, n_op)),
+            pltpu.SemaphoreType.DMA((sectors, 3)),
+            pltpu.SemaphoreType.DMA((sectors, 3)),
             pltpu.SemaphoreType.DMA((sectors, n_sec)),
             pltpu.SemaphoreType.DMA((sectors, n_sec)),
             pltpu.SemaphoreType.DMA((sectors,)),

time: 68.3 us -> 67.2 us (0.984)
  Pallas kernels: 65 us -> 63.9 us
    pallas_call x1, Pallas kernels: 65 us -> 63.9 us  [shards(): pl.pallas_call(functools.partial(kernel, n_op, n_sec), out_shape=jax.Shap...]
where the time goes in v6:
time: 67.2 us; the launch traced here: 67.1 us
  Pallas kernels  63.9 us (95%)
  local copies, waits for them, and re-layouts  3.14 us (5%)
    pallas_call x1, Pallas kernels, shards(): pl.pallas_call(functools.partial(kernel, n_op, n_sec), out_shape=jax.Shap...  63.9 us
    unnamed x5, local copies, waits for them, and re-layouts  1.98 us

profile of v6, /device:TPU:1, one launch (start us, length us, event | category | flops | bytes accessed | tf_op | source)
XLA Modules:
  0.0 67.1 jit_solution(16196913729888415547)
XLA Ops:
  0.0 0.0 copy-start
  0.0 0.0 copy-start.1
  0.0 2.0 %copy.8 = bf16[4,256,4,256]{3,1,2,0:T(8,128)(2,1)S(1)} copy(bf16[4,256,4,256]{3,2,1,0:T(4,128)(2,1)} %param.5) | data formatting | bytes 4194304 | tf_op args[0]
  2.0 0.0 copy-done
  2.0 0.0 copy-done.1
  2.0 63.9 %shard_map.55 = bf16[4,64,1024]{2,1,0:T(8,128)(2,1)S(1)} custom-call(f32[4,4,32]{2,1,0:T(4,128)S(1)} %bitcast.7, s32[32]{0:T(128)S(1)} %copy-done.1, bf16[4,4,256,256]{3,2,1,0:T(8,128)(2,1)S(1)} %bitcast.6, bf16[8,4,256,256]{3,2,1,0:T(8,128)(2,1)} %bitcast.8, bf16[4,8,256,256]{3,2,1,0:T(8,128)(2,1)} %bitcast.9), custom_call_target="tpu_custom_call" | custom-call | flops 8589934592 | bytes 12582912 | tf_op jit(solution)/shard_map/pallas_call | solution.py:269
  65.9 1.2 %reshape.11 = bf16[4,64,4,256]{3,2,1,0:T(4,128)(2,1)} reshape(bf16[4,64,1024]{2,1,0:T(8,128)(2,1)S(1)} %shard_map.55) | data formatting | bytes 1048576 | tf_op jit(solution)/shard_map/reshape | solution.py:302
Async XLA Ops:
  0.0 2.0 %copy-start = (f32[32,4,4]{0,2,1:T(4,128)S(1)}, f32[32,4,4]{0,2,1:T(4,128)}, u32[]{:S(2)}) copy-start(f32[32,4,4]{0,2,1:T(4,128)} %param.9) | copy-start | bytes 6148
  0.0 2.0 %copy-start.1 = (s32[32]{0:T(128)S(1)}, s32[32]{0:T(128)}, u32[]{:S(2)}) copy-start(s32[32]{0:T(128)} %dims_ref.1) | copy-start | bytes 388

commit v7 on v6

--- a/solution.py
+++ b/solution.py
@@ -10,12 +10,12 @@
 MESH = pl.DeviceIdType.MESH
 MIB = 1024 * 1024
 AHEAD = 4
-CHUNK = 64
+CHUNK = 16
 
 
 def kernel(
     n_op, n_sec, site_ref, dims_ref, psi_hbm, left_hbm, right_hbm, out_ref,
-    psi, right, left, mixed, total, zsend, zrecv, relayed,
+    psi, right, left, mixed, total, zsend, zrecv, relayed, turned,
     psi_sem, right_sem, lsend_sem, lrecv_sem, zsend_sem, zrecv_sem, relay_sem,
 ):
     o = lax.axis_index("op")
@@ -134,28 +134,36 @@
         for p in range(p_size):
             psi[j, p] = psi[j, p] * inside
 
-        def one_term(a, _):
-            block = right[j, a]
+        def right_dot(a, slot):
+            turned[slot] = lax.dot_general(
+                psi[j].reshape(p_size * width, width), right[j, a], (((1,), (1,)), ((), ())),
+                preferred_element_type=jnp.float32,
+            )
+
+        def site_mix(a, slot):
             term = a * n_sec + z
             weights = [[site_ref[q, p, term] for p in range(p_size)] for q in range(p_size)]
-            got = lax.dot_general(
-                psi[j].reshape(p_size * width, width), block, (((1,), (1,)), ((), ())),
-                preferred_element_type=jnp.float32,
-            )
             for c in range(width // CHUNK):
+                here = pl.ds(c * CHUNK, CHUNK)
                 parts = [
-                    got[p * width + c * CHUNK:p * width + (c + 1) * CHUNK] for p in range(p_size)
+                    turned[slot, pl.ds(p * width + c * CHUNK, CHUNK), :] for p in range(p_size)
                 ]
                 for q in range(p_size):
                     value = weights[q][0] * parts[0]
                     for p in range(1, p_size):
                         value = value + weights[q][p] * parts[p]
-                    mixed[j, a, pl.ds(c * CHUNK, CHUNK), pl.ds(q * width, width)] = value.astype(
-                        jnp.bfloat16
-                    )
+                    mixed[j, a, here, pl.ds(q * width, width)] = value.astype(jnp.bfloat16)
+
+        def two_terms(i, _):
+            a = 2 * i
+            right_dot(a + 1, 1)
+            site_mix(a, 0)
+            right_dot(lax.rem(a + 2, n_op), 0)
+            site_mix(a + 1, 1)
             return 0
 
-        lax.fori_loop(0, n_op, one_term, 0)
+        right_dot(0, 0)
+        lax.fori_loop(0, n_op // 2, two_terms, 0)
 
     def send_parts(j, which):
         if which == "none":
@@ -286,6 +294,7 @@
             pltpu.VMEM((sectors, width, wide), jnp.bfloat16),
             pltpu.VMEM((sectors, n_sec, rows, wide), jnp.bfloat16),
             pltpu.VMEM((sectors, rows, wide), jnp.bfloat16),
+            pltpu.VMEM((2, wide, width), jnp.float32),
             pltpu.SemaphoreType.DMA((sectors,)),
             pltpu.SemaphoreType.DMA((sectors,)),
             pltpu.SemaphoreType.DMA((sectors, 3)),

time: 67.2 us -> 67.2 us (level)
  no operation moved by 1% of the time
where the time goes in v7:
time: 67.2 us; the launch traced here: 67.1 us
  Pallas kernels  63.9 us (95%)
  local copies, waits for them, and re-layouts  3.14 us (5%)
    pallas_call x1, Pallas kernels, shards(): pl.pallas_call(functools.partial(kernel, n_op, n_sec), out_shape=jax.Shap...  63.9 us
    unnamed x5, local copies, waits for them, and re-layouts  1.98 us

profile of v7, /device:TPU:1, one launch (start us, length us, event | category | flops | bytes accessed | tf_op | source)
XLA Modules:
  0.0 67.1 jit_solution(38957471219651433)
XLA Ops:
  0.0 0.0 copy-start
  0.0 0.0 copy-start.1
  0.0 2.0 %copy.8 = bf16[4,256,4,256]{3,1,2,0:T(8,128)(2,1)S(1)} copy(bf16[4,256,4,256]{3,2,1,0:T(4,128)(2,1)} %param.5) | data formatting | bytes 4194304 | tf_op args[0]
  2.0 0.0 copy-done
  2.0 0.0 copy-done.1
  2.0 63.9 %shard_map.55 = bf16[4,64,1024]{2,1,0:T(8,128)(2,1)S(1)} custom-call(f32[4,4,32]{2,1,0:T(4,128)S(1)} %bitcast.7, s32[32]{0:T(128)S(1)} %copy-done.1, bf16[4,4,256,256]{3,2,1,0:T(8,128)(2,1)S(1)} %bitcast.6, bf16[8,4,256,256]{3,2,1,0:T(8,128)(2,1)} %bitcast.8, bf16[4,8,256,256]{3,2,1,0:T(8,128)(2,1)} %bitcast.9), custom_call_target="tpu_custom_call" | custom-call | flops 8589934592 | bytes 12582912 | tf_op jit(solution)/shard_map/pallas_call | solution.py:277
  65.9 1.2 %reshape.11 = bf16[4,64,4,256]{3,2,1,0:T(4,128)(2,1)} reshape(bf16[4,64,1024]{2,1,0:T(8,128)(2,1)S(1)} %shard_map.55) | data formatting | bytes 1048576 | tf_op jit(solution)/shard_map/reshape | solution.py:311
Async XLA Ops:
  0.0 2.0 %copy-start = (f32[32,4,4]{0,2,1:T(4,128)S(1)}, f32[32,4,4]{0,2,1:T(4,128)}, u32[]{:S(2)}) copy-start(f32[32,4,4]{0,2,1:T(4,128)} %param.9) | copy-start | bytes 6148
  0.0 2.0 %copy-start.1 = (s32[32]{0:T(128)S(1)}, s32[32]{0:T(128)}, u32[]{:S(2)}) copy-start(s32[32]{0:T(128)} %dims_ref.1) | copy-start | bytes 388

commit v8 on v7

--- a/solution.py
+++ b/solution.py
@@ -9,7 +9,7 @@
 
 MESH = pl.DeviceIdType.MESH
 MIB = 1024 * 1024
-AHEAD = 4
+AHEAD = 6
 CHUNK = 16
 
 

time: 67.2 us -> 67.2 us (level)
  no operation moved by 1% of the time
where the time goes in v8:
time: 67.2 us; the launch traced here: 67.1 us
  Pallas kernels  63.9 us (95%)
  local copies, waits for them, and re-layouts  3.14 us (5%)
    pallas_call x1, Pallas kernels, shards(): pl.pallas_call(functools.partial(kernel, n_op, n_sec), out_shape=jax.Shap...  63.9 us
    unnamed x5, local copies, waits for them, and re-layouts  1.98 us

profile of v8, /device:TPU:1, one launch (start us, length us, event | category | flops | bytes accessed | tf_op | source)
XLA Modules:
  0.0 67.1 jit_solution(5443008615780606533)
XLA Ops:
  0.0 0.0 copy-start
  0.0 0.0 copy-start.1
  0.0 2.0 %copy.8 = bf16[4,256,4,256]{3,1,2,0:T(8,128)(2,1)S(1)} copy(bf16[4,256,4,256]{3,2,1,0:T(4,128)(2,1)} %param.5) | data formatting | bytes 4194304 | tf_op args[0]
  2.0 0.0 copy-done
  2.0 0.0 copy-done.1
  2.0 63.9 %shard_map.55 = bf16[4,64,1024]{2,1,0:T(8,128)(2,1)S(1)} custom-call(f32[4,4,32]{2,1,0:T(4,128)S(1)} %bitcast.7, s32[32]{0:T(128)S(1)} %copy-done.1, bf16[4,4,256,256]{3,2,1,0:T(8,128)(2,1)S(1)} %bitcast.6, bf16[8,4,256,256]{3,2,1,0:T(8,128)(2,1)} %bitcast.8, bf16[4,8,256,256]{3,2,1,0:T(8,128)(2,1)} %bitcast.9), custom_call_target="tpu_custom_call" | custom-call | flops 8589934592 | bytes 12582912 | tf_op jit(solution)/shard_map/pallas_call | solution.py:277
  65.9 1.2 %reshape.11 = bf16[4,64,4,256]{3,2,1,0:T(4,128)(2,1)} reshape(bf16[4,64,1024]{2,1,0:T(8,128)(2,1)S(1)} %shard_map.55) | data formatting | bytes 1048576 | tf_op jit(solution)/shard_map/reshape | solution.py:311
Async XLA Ops:
  0.0 2.0 %copy-start = (f32[32,4,4]{0,2,1:T(4,128)S(1)}, f32[32,4,4]{0,2,1:T(4,128)}, u32[]{:S(2)}) copy-start(f32[32,4,4]{0,2,1:T(4,128)} %param.9) | copy-start | bytes 6148
  0.0 2.0 %copy-start.1 = (s32[32]{0:T(128)S(1)}, s32[32]{0:T(128)}, u32[]{:S(2)}) copy-start(s32[32]{0:T(128)} %dims_ref.1) | copy-start | bytes 388
